TPU v7x, 256 devices: a whole 4x4x8 slice. The times are simulated.
256 devices in a mesh: section: 8 (over x, y_hi), dp: 32 (over z, y_lo, core).
Axes of the slice: x: 4, y: 4 (y_hi: 2, y_lo: 2; y = y_hi * 2 + y_lo), z: 8, core: 2. Of those that a mesh axis runs over, the one named last changes fastest.
Arguments:
- train_acts: bfloat16 [8, 5888, 27648], P('section', 'dp'), may hold values from -6 to 6
- train_grads: bfloat16 [8, 5888, 5120], P('section', 'dp'), may hold values from -0.011962891 to 0.011962891
- train_ids: int32 [5888], P('dp'), may hold values from 0 to 255, as said below
- val_acts: bfloat16 [8, 256, 27648], P('section', 'dp'), may hold values from -6 to 6
- val_grads: bfloat16 [8, 256, 5120], P('section', 'dp'), may hold values from -0.011962891 to 0.011962891
- val_ids: int32 [256], P('dp'), may hold values from 0 to 15, never falling along the last dimension, each value on 1 to 32 neighbouring positions
Outputs:
- scores: float32 [256, 16], P('dp', 'section')
Inputs may be any that keep to these rules, and one draw needn't show every extreme that they name: `train_ids`: the training tokens of rows k * 184 to (k + 1) * 184 - 1 belong to sequences k * 8 to (k + 1) * 8 - 1, in non-decreasing order, each of these sequences with one token or more. `val_ids`: validation sequence numbers never fall along the tokens; each sequence has 1 to 32 tokens.
All inputs are finite; a program needn't handle non-finite values.
Results may differ from a plain program's by a relative error of at most 0.0003.
Values may be sent and summed in bfloat16 or wider, within the bound.
No kernel may reach another device: no remote copies, remote signals or barrier semaphores. Data moves between devices by JAX's collectives and lax.ppermute only.
A program may use at most 128 MiB of HBM per device.

v0:
```python
import functools

import jax
import jax.numpy as jnp
from jax import lax
from jax.experimental import pallas as pl
from jax.experimental.pallas import tpu as pltpu
from jax.sharding import Mesh, PartitionSpec as P

SEQ_DEV = 8
VAL_SEQS = 16
LANES = 128
ACT_TILES = 2
FETCH_MIB = 22
LATE_MIB = 8
MIRROR = (0, 2, 1, 4, 3, 6, 5, 7, 8, 10, 9, 14, 15, 13, 11, 12)
F32 = jnp.float32
HIGHEST = lax.Precision.HIGHEST


def contract(left, piece):
    return lax.dot_general(left, piece, (((1,), (1,)), ((), ())), preferred_element_type=F32)


def grams(train, blocks, act_width, grad_width):
    tile = act_width // ACT_TILES
    starts = [(i * tile, tile) for i in range(ACT_TILES)] + [(act_width, grad_width)]
    parts = []
    for start, size in starts:
        piece = jnp.concatenate([block[:, start : start + size] for block in blocks], axis=0)
        parts.append(contract(train[:, start : start + size], piece))
    return sum(parts[1:-1], parts[0]), parts[-1]


def val_onehot(blocks):
    width = blocks[0].shape[1]
    numbers = [block[:, width - LANES :].astype(F32)[:, :VAL_SEQS] for block in blocks]
    stacked = jnp.concatenate(numbers, axis=0)
    return (stacked == lax.broadcasted_iota(jnp.int32, stacked.shape, 1).astype(F32)).astype(F32)


def fetch_kernel(act_width, grad_width, *refs):
    core, sources = refs[0][0], (refs[1:3], refs[3:5])
    blocks, (own, partner, stack, sems, val_sems) = refs[5:-5], refs[-5:]
    copies = [
        pltpu.make_async_copy(block, stack.at[i], val_sems.at[i]) for i, block in enumerate(blocks)
    ]
    for k, (pair, target) in enumerate(zip(sources, (own, partner))):
        begin = 0
        for j, (source, size) in enumerate(zip(pair, (act_width, grad_width))):
            held = source.at[0, :, pl.ds(pl.multiple_of(core * size, LANES), size)]
            copies.append(
                pltpu.make_async_copy(held, target.at[:, begin : begin + size], sems.at[k, j])
            )
            begin += size
    for copy in copies:
        copy.start()
    for copy in copies:
        copy.wait()


def gram_kernel(act_width, grad_width, rows, partner, stack, *refs):
    late, (kept, sent, hot) = refs[:-3], refs[-3:]
    blocks = [stack.at[i] for i in range(stack.shape[0])] + list(late)
    mirrored = [blocks[i] for i in MIRROR]
    sent[0], sent[1] = grams(partner, mirrored, act_width, grad_width)
    kept[0], kept[1] = grams(rows, blocks, act_width, grad_width)
    hot[...] = val_onehot(blocks)


def score_kernel(ids, kept, came, hot, out):
    product = (kept[0] + came[0]) * (kept[1] + came[1])
    by_val = jnp.dot(product, hot[...], precision=HIGHEST, preferred_element_type=F32)
    places = lax.broadcasted_iota(jnp.int32, (SEQ_DEV, ids.shape[1]), 0)
    onehot = (ids[...] == places).astype(F32)
    out[...] = jnp.dot(onehot, by_val, precision=HIGHEST, preferred_element_type=F32)


def call(kernel, spaces, shapes, operands, mebibytes, scratch=(), flops=0):
    return pl.pallas_call(
        kernel,
        in_specs=[pl.BlockSpec(memory_space=space) for space in spaces],
        out_specs=[pl.BlockSpec(memory_space=pltpu.VMEM)] * len(shapes),
        out_shape=[jax.ShapeDtypeStruct(shape, dtype) for shape, dtype in shapes],
        scratch_shapes=list(scratch),
        compiler_params=pltpu.CompilerParams(vmem_limit_bytes=mebibytes * 1024 * 1024),
        cost_estimate=pl.CostEstimate(flops=flops, bytes_accessed=0, transcendentals=0),
    )(*operands)


def after(block, *done):
    return lax.optimization_barrier((block, *done))[0]


def on_device(train_acts, train_grads, train_ids, val_acts, val_grads, val_ids):
    tokens = train_acts.shape[1]
    act_width, grad_width = train_acts.shape[2] // 2, train_grads.shape[2] // 2
    both = ("zy", "core")
    places = lax.axis_size("zy") * 2
    sections = lax.axis_size("section")
    core = lax.axis_index("core")

    def mover(target):
        pairs = [(i, target(i) % places) for i in range(places)]
        return lambda block: lax.ppermute(block, both, pairs)

    ahead = mover(lambda i: i + 4 if i % 2 == 0 else i - 4)
    back = mover(lambda i: i - 4 if i % 2 == 0 else i + 4)
    beside = mover(lambda i: i ^ 2)
    other_core = mover(lambda i: i ^ 1)

    def columns(acts, grads, which):
        return [
            lax.dynamic_slice_in_dim(acts[0], which * act_width, act_width, 1),
            lax.dynamic_slice_in_dim(grads[0], which * grad_width, grad_width, 1),
        ]

    numbers = jnp.broadcast_to(val_ids.astype(jnp.bfloat16)[:, None], (SEQ_DEV, LANES))
    mine = jnp.concatenate([*columns(val_acts, val_grads, core), numbers], axis=1)
    theirs = jnp.concatenate([*columns(val_acts, val_grads, 1 - core), numbers], axis=1)
    own, other = {}, {}
    other_grads = other_core(train_grads)
    came = other_core(after(theirs, other_grads))
    first = core == 0
    own[0] = jnp.concatenate(
        [jnp.where(first, mine, came), jnp.where(first, came, mine)], axis=0
    )

    other_acts = other_core(after(train_acts, own[0]))
    own[-1] = ahead(own[0])
    other[0] = beside(own[0])
    own[1] = back(own[0])
    own[-2] = ahead(after(own[-1], other[0]))
    other[1] = beside(own[1])
    own[2] = back(own[1])
    own[-3] = ahead(own[-2])
    other[-2] = beside(after(own[-2], other[0]))
    own[3] = back(own[2])
    own[4] = ahead(after(own[-3], other[1]))
    other[-3] = beside(after(own[-3], other[1]))
    other[2] = back(after(other[1], own[3]))
    late = [
        beside(after(own[4], other[-2])),
        ahead(after(other[0], own[4], other[-2])),
        back(after(other[2], other[-3])),
    ]
    early = [own[d] for d in (0, -1, 1, -2, 2, -3, 3, 4)] + [other[d] for d in (0, -2, 2, 1, -3)]

    vmem, hbm = pltpu.VMEM, pltpu.HBM
    cost = 4 * tokens * 256 * (act_width + grad_width)
    rows_shape = ((tokens, act_width + grad_width), train_acts.dtype)

    widths = (act_width, grad_width)
    stack_shape = ((len(early), *own[0].shape), own[0].dtype)
    gram_shape = ((2, tokens, len(MIRROR) * own[0].shape[0]), F32)
    hot_shape = ((len(MIRROR) * own[0].shape[0], VAL_SEQS), F32)
    rows, partner, stack = call(
        functools.partial(fetch_kernel, *widths),
        [pltpu.SMEM] + [hbm] * (4 + len(early)),
        [rows_shape, rows_shape, stack_shape],
        [core.reshape(1), train_acts, train_grads, other_acts, other_grads, *early],
        FETCH_MIB,
        [pltpu.SemaphoreType.DMA((2, 2)), pltpu.SemaphoreType.DMA((len(early),))],
    )
    kept, sent, hot = call(
        functools.partial(gram_kernel, *widths),
        [vmem] * (3 + len(late)),
        [gram_shape, gram_shape, hot_shape],
        [rows, partner, stack, *late],
        LATE_MIB,
        (),
        cost,
    )
    local_ids = train_ids - (lax.axis_index("zy") * 2 + core) * SEQ_DEV
    operands = [local_ids[None, :], kept, other_core(sent), hot]
    (score,) = call(
        score_kernel, [vmem] * len(operands), [((SEQ_DEV, VAL_SEQS), F32)], operands, LATE_MIB
    )
    share = VAL_SEQS // sections
    parts = score.reshape(SEQ_DEV, sections, share).transpose(1, 0, 2)
    return jnp.sum(lax.all_to_all(parts, "section", 0, 0, tiled=True), axis=0)


def solution(mesh):
    cores = 2
    sections, rest = mesh.devices.shape
    grid = Mesh(mesh.devices.reshape(sections, rest // cores, cores), ("section", "zy", "core"))
    both = ("zy", "core")
    return jax.shard_map(
        on_device,
        mesh=grid,
        in_specs=(
            P("section", both, None),
            P("section", both, None),
            P(both),
            P("section", both, None),
            P("section", both, None),
            P(both),
        ),
        out_specs=P(both, "section"),
        check_vma=False,
    )
```

profile of v0, /device:TPU:8, one launch (start us, length us, event | category | flops | bytes accessed | tf_op | source)
XLA Modules:
  0.0 105.0 jit_solution(12512651779068614519)
XLA Ops:
  0.0 0.7 convert_element_type.3
  0.7 1.1 %dynamic-slice_bitcast_fusion.1 = (bf16[8,13824]{1,0:T(8,128)(2,1)S(1)}, bf16[8,13824]{1,0:T(8,128)(2,1)S(1)}) fusion(bf16[1,8,27648]{2,1,0:T(8,128)(2,1)} %param.9, s32[]{:T(128)S(6)} %select_n.25, s32[]{:T(128)S(6)} %select_n.27), kind=kLoop, calls=%fused_computation.6 | loop fusion | bytes 884744 | tf_op jit(solution)/shard_map/dynamic_slice | solution.py:114
  1.7 0.8 dynamic-slice_bitcast_fusion.3
  2.6 1.4 %collective-permute-done.refs_4_ = bf16[1,184,5120]{2,1,0:T(8,128)(2,1)S(1)} collective-permute-done((bf16[1,184,5120]{2,1,0:T(8,128)(2,1)}, bf16[1,184,5120]{2,1,0:T(8,128)(2,1)S(1)}, u32[]{:S(2)}, u32[]{:S(2)}) %collective-permute-start) | collective-permute-done | bytes 1884192 | tf_op jit(solution)/shard_map/ppermute | solution.py:105
  4.2 1.4 %collective-permute-done.1 = bf16[8,16512]{1,0:T(8,128)(2,1)S(1)} collective-permute-done((bf16[8,16512]{1,0:T(8,128)(2,1)S(1)}, bf16[8,16512]{1,0:T(8,128)(2,1)S(1)}, u32[]{:S(2)}, u32[]{:S(2)}) %collective-permute-start.1) | collective-permute-done | bytes 264224 | tf_op jit(solution)/shard_map/ppermute | solution.py:105
  5.8 0.2 collective-permute-start.2
  6.0 1.9 %collective-permute-start.3 = (bf16[16,16512]{1,0:T(8,128)(2,1)S(1)}, bf16[16,16512]{1,0:T(8,128)(2,1)S(1)}, u32[]{:S(2)}, u32[]{:S(2)}) collective-permute-start(bf16[16,16512]{1,0:T(8,128)(2,1)S(1)} %pad_maximum_fusion.refs_5_), channel_id=1, source_target_pairs={{0,4},{1,29},{2,6},{3,31},{4,8},{5,1},{6,10},{7,3},{8,12},{9,5},{1... | collective-permute-start | bytes 1585160 | tf_op jit(solution)/shard_map/ppermute | solution.py:105
  7.9 0.4 collective-permute-start.5
  8.4 4.0 %collective-permute-start.4 = (bf16[16,16512]{1,0:T(8,128)(2,1)S(1)}, bf16[16,16512]{1,0:T(8,128)(2,1)S(1)}, u32[]{:S(2)}, u32[]{:S(2)}) collective-permute-start(bf16[16,16512]{1,0:T(8,128)(2,1)S(1)} %pad_maximum_fusion.refs_5_), channel_id=1, source_target_pairs={{0,28},{1,5},{2,30},{3,7},{4,0},{5,9},{6,2},{7,11},{8,4},{9,13},{1... | collective-permute-start | bytes 1585160 | tf_op jit(solution)/shard_map/ppermute | solution.py:105
  12.4 9.8 %collective-permute-done.3.refs_6_ = bf16[16,16512]{1,0:T(8,128)(2,1)S(1)} collective-permute-done((bf16[16,16512]{1,0:T(8,128)(2,1)S(1)}, bf16[16,16512]{1,0:T(8,128)(2,1)S(1)}, u32[]{:S(2)}, u32[]{:S(2)}) %collective-permute-start.3) | collective-permute-done | bytes 528416 | tf_op jit(solution)/shard_map/ppermute | solution.py:105
  22.1 0.4 collective-permute-start.6
  22.5 1.2 %collective-permute-done.4.refs_7_ = bf16[16,16512]{1,0:T(8,128)(2,1)S(1)} collective-permute-done((bf16[16,16512]{1,0:T(8,128)(2,1)S(1)}, bf16[16,16512]{1,0:T(8,128)(2,1)S(1)}, u32[]{:S(2)}, u32[]{:S(2)}) %collective-permute-start.4) | collective-permute-done | bytes 528416 | tf_op jit(solution)/shard_map/ppermute | solution.py:105
  23.7 3.7 %collective-permute-start.7 = (bf16[16,16512]{1,0:T(8,128)(2,1)S(1)}, bf16[16,16512]{1,0:T(8,128)(2,1)S(1)}, u32[]{:S(2)}, u32[]{:S(2)}) collective-permute-start(bf16[16,16512]{1,0:T(8,128)(2,1)S(1)} %collective-permute-done.4.refs_7_), channel_id=1, source_target_pairs={{0,28},{1,5},{2,30},{3,7},{4,0},{5,9},{6,2},{7,11},{8,4},{9,13},{1... | collective-permute-start | bytes 1585160 | tf_op jit(solution)/shard_map/ppermute | solution.py:105
  27.3 0.4 collective-permute-start.10
  27.8 9.5 %collective-permute-done.6.refs_8_ = bf16[16,16512]{1,0:T(8,128)(2,1)S(1)} collective-permute-done((bf16[16,16512]{1,0:T(8,128)(2,1)S(1)}, bf16[16,16512]{1,0:T(8,128)(2,1)S(1)}, u32[]{:S(2)}, u32[]{:S(2)}) %collective-permute-start.6) | collective-permute-done | bytes 528416 | tf_op jit(solution)/shard_map/ppermute | solution.py:105
  37.3 1.0 collective-permute-done.7.refs_9_
  38.3 3.7 %collective-permute-start.9 = (bf16[16,16512]{1,0:T(8,128)(2,1)S(1)}, bf16[16,16512]{1,0:T(8,128)(2,1)S(1)}, u32[]{:S(2)}, u32[]{:S(2)}) collective-permute-start(bf16[16,16512]{1,0:T(8,128)(2,1)S(1)} %collective-permute-done.7.refs_9_), channel_id=1, source_target_pairs={{0,28},{1,5},{2,30},{3,7},{4,0},{5,9},{6,2},{7,11},{8,4},{9,13},{1... | collective-permute-start | bytes 1585160 | tf_op jit(solution)/shard_map/ppermute | solution.py:105
  42.0 0.4 collective-permute-start.12
  42.5 9.3 %collective-permute-done.8.refs_10_ = bf16[16,16512]{1,0:T(8,128)(2,1)S(1)} collective-permute-done((bf16[16,16512]{1,0:T(8,128)(2,1)S(1)}, bf16[16,16512]{1,0:T(8,128)(2,1)S(1)}, u32[]{:S(2)}, u32[]{:S(2)}) %collective-permute-start.8) | collective-permute-done | bytes 528416 | tf_op jit(solution)/shard_map/ppermute | solution.py:105
  51.8 0.5 collective-permute-start.14
  52.2 3.6 %collective-permute-start.13 = (bf16[16,16512]{1,0:T(8,128)(2,1)S(1)}, bf16[16,16512]{1,0:T(8,128)(2,1)S(1)}, u32[]{:S(2)}, u32[]{:S(2)}) collective-permute-start(bf16[16,16512]{1,0:T(8,128)(2,1)S(1)} %collective-permute-done.10.refs_16_), channel_id=1, source_target_pairs={{0,28},{1,5},{2,30},{3,7},{4,0},{5,9},{6,2},{7,11},{8,4},{9,13},{1... | collective-permute-start | bytes 1585160 | tf_op jit(solution)/shard_map/ppermute | solution.py:105
  55.8 11.4 %collective-permute-done.11.refs_12_ = bf16[16,16512]{1,0:T(8,128)(2,1)S(1)} collective-permute-done((bf16[16,16512]{1,0:T(8,128)(2,1)S(1)}, bf16[16,16512]{1,0:T(8,128)(2,1)S(1)}, u32[]{:S(2)}, u32[]{:S(2)}) %collective-permute-start.11) | collective-permute-done | bytes 528416 | tf_op jit(solution)/shard_map/ppermute | solution.py:105
  67.2 3.5 %collective-permute-start.17 = (bf16[16,16512]{1,0:T(8,128)(2,1)S(1)}, bf16[16,16512]{1,0:T(8,128)(2,1)S(1)}, u32[]{:S(2)}, u32[]{:S(2)}) collective-permute-start(bf16[16,16512]{1,0:T(8,128)(2,1)S(1)} %collective-permute-done.13.refs_15_), channel_id=1, source_target_pairs={{0,28},{1,5},{2,30},{3,7},{4,0},{5,9},{6,2},{7,11},{8,4},{9,13},{1... | collective-permute-start | bytes 1585160 | tf_op jit(solution)/shard_map/ppermute | solution.py:105
  70.7 3.9 %copy-done.1 = bf16[1,184,27648]{2,1,0:T(8,128)(2,1)} copy-done((bf16[1,184,27648]{2,1,0:T(8,128)(2,1)}, bf16[1,184,27648]{2,1,0:T(8,128)(2,1)S(1)}, u32[]{:S(2)}) %copy-start.1) | copy-done | bytes 10174488
  74.6 1.5 %copy-done = bf16[1,184,5120]{2,1,0:T(8,128)(2,1)S(1)} copy-done((bf16[1,184,5120]{2,1,0:T(8,128)(2,1)S(1)}, bf16[1,184,5120]{2,1,0:T(8,128)(2,1)}, u32[]{:S(2)}) %copy-start) | copy-done | bytes 1884184
  76.1 4.7 %shard_map.64 = (bf16[184,16384]{1,0:T(8,128)(2,1)S(1)}, bf16[184,16384]{1,0:T(8,128)(2,1)S(1)}, bf16[13,16,16512]{2,1,0:T(8,128)(2,1)S(1)}) custom-call(s32[1]{0:T(128)} %bitcast.1.refs_0_, bf16[1,184,27648]{2,1,0:T(8,128)(2,1)} %refs_1_.1, bf16[1,184,5120]{2,1,0:T(8,128)(2,1)S(1)} %copy-done, bf16[1,184,27648]{2,1,0:T(8,128)(2,1)} %copy-done.1, ...), custom_call_target="tpu_custom_call" | custom-call | tf_op jit(solution)/shard_map/pallas_call | solution.py:80
  80.8 2.1 %collective-permute-done.16.refs_1_ = bf16[16,16512]{1,0:T(8,128)(2,1)S(1)} collective-permute-done((bf16[16,16512]{1,0:T(8,128)(2,1)S(1)}, bf16[16,16512]{1,0:T(8,128)(2,1)S(1)}, u32[]{:S(2)}, u32[]{:S(2)}) %collective-permute-start.16) | collective-permute-done | bytes 528416 | tf_op jit(solution)/shard_map/ppermute | solution.py:105
  82.8 5.6 %shard_map.65 = (f32[2,184,256]{2,1,0:T(8,128)S(1)}, f32[2,184,256]{2,1,0:T(8,128)S(1)}, f32[256,16]{1,0:T(8,128)S(1)}) custom-call(bf16[184,16384]{1,0:T(8,128)(2,1)S(1)} %get-tuple-element.26.rows, bf16[184,16384]{1,0:T(8,128)(2,1)S(1)} %get-tuple-element.27.partner, bf16[13,16,16512]{2,1,0:T(8,128)(2,1)S(1)} %get-tuple-element.28.stack, ...), custom_call_target="tpu_custom_call" | custom-call | flops 3087007744 | tf_op jit(solution)/shard_map/pallas_call | solution.py:80
  88.5 1.7 %collective-permute-done.18.came = f32[2,184,256]{2,1,0:T(8,128)S(1)} collective-permute-done((f32[2,184,256]{2,1,0:T(8,128)S(1)}, f32[2,184,256]{2,1,0:T(8,128)S(1)}, u32[]{:S(2)}, u32[]{:S(2)}) %collective-permute-start.18) | collective-permute-done | bytes 376864 | tf_op jit(solution)/shard_map/ppermute | solution.py:105
  90.2 0.6 shard_map.66
  90.9 13.5 %all_to_all.5 = f32[8,8,2]{1,2,0:T(2,128)S(1)} all-to-all(f32[8,8,2]{1,2,0:T(2,128)S(1)} %bitcast.14), channel_id=1, replica_groups=mesh['section'=8,'zy'=16,'core'=2] {'section'}, dimensions={0} | all-to-all | bytes 1024 | tf_op jit(solution)/shard_map/all_to_all | solution.py:181
  104.4 0.6 reduce_sum.9
  (26 shorter events, 0.6 us)
Async XLA Ops:
  0.0 4.1 %collective-permute-start = (bf16[1,184,5120]{2,1,0:T(8,128)(2,1)}, bf16[1,184,5120]{2,1,0:T(8,128)(2,1)S(1)}, u32[]{:S(2)}, u32[]{:S(2)}) collective-permute-start(bf16[1,184,5120]{2,1,0:T(8,128)(2,1)} %refs_2_.1), channel_id=1, source_target_pairs={{0,1},{1,0},{2,3},{3,2},{4,5},{5,4},{6,7},{7,6},{8,9},{9,8},{10,11... | collective-permute-start | bytes 5652488 | tf_op jit(solution)/shard_map/ppermute | solution.py:105
  4.1 1.5 %collective-permute-start.1 = (bf16[8,16512]{1,0:T(8,128)(2,1)S(1)}, bf16[8,16512]{1,0:T(8,128)(2,1)S(1)}, u32[]{:S(2)}, u32[]{:S(2)}) collective-permute-start(bf16[8,16512]{1,0:T(8,128)(2,1)S(1)} %pad_maximum_fusion.1), channel_id=1, source_target_pairs={{0,1},{1,0},{2,3},{3,2},{4,5},{5,4},{6,7},{7,6},{8,9},{9,8},{10,11... | collective-permute-start | bytes 792584 | tf_op jit(solution)/shard_map/ppermute | solution.py:105
  5.8 64.9 %collective-permute-start.2 = (bf16[1,184,27648]{2,1,0:T(8,128)(2,1)}, bf16[1,184,27648]{2,1,0:T(8,128)(2,1)S(1)}, u32[]{:S(2)}, u32[]{:S(2)}) collective-permute-start(bf16[1,184,27648]{2,1,0:T(8,128)(2,1)} %refs_1_.1), channel_id=1, source_target_pairs={{0,1},{1,0},{2,3},{3,2},{4,5},{5,4},{6,7},{7,6},{8,9},{9,8},{10,11... | collective-permute-start | bytes 30523400 | tf_op jit(solution)/shard_map/ppermute | solution.py:105
  6.0 16.1 %collective-permute-start.3 = (bf16[16,16512]{1,0:T(8,128)(2,1)S(1)}, bf16[16,16512]{1,0:T(8,128)(2,1)S(1)}, u32[]{:S(2)}, u32[]{:S(2)}) collective-permute-start(bf16[16,16512]{1,0:T(8,128)(2,1)S(1)} %pad_maximum_fusion.refs_5_), channel_id=1, source_target_pairs={{0,4},{1,29},{2,6},{3,31},{4,8},{5,1},{6,10},{7,3},{8,12},{9,5},{1... | collective-permute-start | bytes 1585160 | tf_op jit(solution)/shard_map/ppermute | solution.py:105
  7.9 14.2 %collective-permute-start.5 = (bf16[16,16512]{1,0:T(8,128)(2,1)S(1)}, bf16[16,16512]{1,0:T(8,128)(2,1)S(1)}, u32[]{:S(2)}, u32[]{:S(2)}) collective-permute-start(bf16[16,16512]{1,0:T(8,128)(2,1)S(1)} %pad_maximum_fusion.refs_5_), channel_id=1, source_target_pairs={{0,2},{1,3},{2,0},{3,1},{4,6},{5,7},{6,4},{7,5},{8,10},{9,11},{10,... | collective-permute-start | bytes 1585160 | tf_op jit(solution)/shard_map/ppermute | solution.py:105
  8.4 15.3 %collective-permute-start.4 = (bf16[16,16512]{1,0:T(8,128)(2,1)S(1)}, bf16[16,16512]{1,0:T(8,128)(2,1)S(1)}, u32[]{:S(2)}, u32[]{:S(2)}) collective-permute-start(bf16[16,16512]{1,0:T(8,128)(2,1)S(1)} %pad_maximum_fusion.refs_5_), channel_id=1, source_target_pairs={{0,28},{1,5},{2,30},{3,7},{4,0},{5,9},{6,2},{7,11},{8,4},{9,13},{1... | collective-permute-start | bytes 1585160 | tf_op jit(solution)/shard_map/ppermute | solution.py:105
  22.1 15.2 %collective-permute-start.6 = (bf16[16,16512]{1,0:T(8,128)(2,1)S(1)}, bf16[16,16512]{1,0:T(8,128)(2,1)S(1)}, u32[]{:S(2)}, u32[]{:S(2)}) collective-permute-start(bf16[16,16512]{1,0:T(8,128)(2,1)S(1)} %collective-permute-done.3.refs_6_), channel_id=1, source_target_pairs={{0,4},{1,29},{2,6},{3,31},{4,8},{5,1},{6,10},{7,3},{8,12},{9,5},{1... | collective-permute-start | bytes 1585160 | tf_op jit(solution)/shard_map/ppermute | solution.py:105
  23.7 14.7 %collective-permute-start.7 = (bf16[16,16512]{1,0:T(8,128)(2,1)S(1)}, bf16[16,16512]{1,0:T(8,128)(2,1)S(1)}, u32[]{:S(2)}, u32[]{:S(2)}) collective-permute-start(bf16[16,16512]{1,0:T(8,128)(2,1)S(1)} %collective-permute-done.4.refs_7_), channel_id=1, source_target_pairs={{0,28},{1,5},{2,30},{3,7},{4,0},{5,9},{6,2},{7,11},{8,4},{9,13},{1... | collective-permute-start | bytes 1585160 | tf_op jit(solution)/shard_map/ppermute | solution.py:105
  27.3 15.1 %collective-permute-start.10 = (bf16[16,16512]{1,0:T(8,128)(2,1)S(1)}, bf16[16,16512]{1,0:T(8,128)(2,1)S(1)}, u32[]{:S(2)}, u32[]{:S(2)}) collective-permute-start(bf16[16,16512]{1,0:T(8,128)(2,1)S(1)} %collective-permute-done.4.refs_7_), channel_id=1, source_target_pairs={{0,2},{1,3},{2,0},{3,1},{4,6},{5,7},{6,4},{7,5},{8,10},{9,11},{10,... | collective-permute-start | bytes 1585160 | tf_op jit(solution)/shard_map/ppermute | solution.py:105
  37.3 14.5 %collective-permute-start.8 = (bf16[16,16512]{1,0:T(8,128)(2,1)S(1)}, bf16[16,16512]{1,0:T(8,128)(2,1)S(1)}, u32[]{:S(2)}, u32[]{:S(2)}) collective-permute-start(bf16[16,16512]{1,0:T(8,128)(2,1)S(1)} %collective-permute-done.6.refs_8_), channel_id=1, source_target_pairs={{0,4},{1,29},{2,6},{3,31},{4,8},{5,1},{6,10},{7,3},{8,12},{9,5},{1... | collective-permute-start | bytes 1585160 | tf_op jit(solution)/shard_map/ppermute | solution.py:105
  38.3 13.9 %collective-permute-start.9 = (bf16[16,16512]{1,0:T(8,128)(2,1)S(1)}, bf16[16,16512]{1,0:T(8,128)(2,1)S(1)}, u32[]{:S(2)}, u32[]{:S(2)}) collective-permute-start(bf16[16,16512]{1,0:T(8,128)(2,1)S(1)} %collective-permute-done.7.refs_9_), channel_id=1, source_target_pairs={{0,28},{1,5},{2,30},{3,7},{4,0},{5,9},{6,2},{7,11},{8,4},{9,13},{1... | collective-permute-start | bytes 1585160 | tf_op jit(solution)/shard_map/ppermute | solution.py:105
  42.0 13.8 %collective-permute-start.12 = (bf16[16,16512]{1,0:T(8,128)(2,1)S(1)}, bf16[16,16512]{1,0:T(8,128)(2,1)S(1)}, u32[]{:S(2)}, u32[]{:S(2)}) collective-permute-start(bf16[16,16512]{1,0:T(8,128)(2,1)S(1)} %collective-permute-done.6.refs_8_), channel_id=1, source_target_pairs={{0,2},{1,3},{2,0},{3,1},{4,6},{5,7},{6,4},{7,5},{8,10},{9,11},{10,... | collective-permute-start | bytes 1585160 | tf_op jit(solution)/shard_map/ppermute | solution.py:105
  51.8 15.4 %collective-permute-start.11 = (bf16[16,16512]{1,0:T(8,128)(2,1)S(1)}, bf16[16,16512]{1,0:T(8,128)(2,1)S(1)}, u32[]{:S(2)}, u32[]{:S(2)}) collective-permute-start(bf16[16,16512]{1,0:T(8,128)(2,1)S(1)} %collective-permute-done.8.refs_10_), channel_id=1, source_target_pairs={{0,4},{1,29},{2,6},{3,31},{4,8},{5,1},{6,10},{7,3},{8,12},{9,5},{1... | collective-permute-start | bytes 1585160 | tf_op jit(solution)/shard_map/ppermute | solution.py:105
  51.8 15.4 %collective-permute-start.14 = (bf16[16,16512]{1,0:T(8,128)(2,1)S(1)}, bf16[16,16512]{1,0:T(8,128)(2,1)S(1)}, u32[]{:S(2)}, u32[]{:S(2)}) collective-permute-start(bf16[16,16512]{1,0:T(8,128)(2,1)S(1)} %collective-permute-done.8.refs_10_), channel_id=1, source_target_pairs={{0,2},{1,3},{2,0},{3,1},{4,6},{5,7},{6,4},{7,5},{8,10},{9,11},{10,... | collective-permute-start | bytes 1585160 | tf_op jit(solution)/shard_map/ppermute | solution.py:105
  52.2 14.9 %collective-permute-start.13 = (bf16[16,16512]{1,0:T(8,128)(2,1)S(1)}, bf16[16,16512]{1,0:T(8,128)(2,1)S(1)}, u32[]{:S(2)}, u32[]{:S(2)}) collective-permute-start(bf16[16,16512]{1,0:T(8,128)(2,1)S(1)} %collective-permute-done.10.refs_16_), channel_id=1, source_target_pairs={{0,28},{1,5},{2,30},{3,7},{4,0},{5,9},{6,2},{7,11},{8,4},{9,13},{1... | collective-permute-start | bytes 1585160 | tf_op jit(solution)/shard_map/ppermute | solution.py:105
  67.2 15.7 %collective-permute-start.16 = (bf16[16,16512]{1,0:T(8,128)(2,1)S(1)}, bf16[16,16512]{1,0:T(8,128)(2,1)S(1)}, u32[]{:S(2)}, u32[]{:S(2)}) collective-permute-start(bf16[16,16512]{1,0:T(8,128)(2,1)S(1)} %collective-permute-done.5.refs_13_), channel_id=1, source_target_pairs={{0,4},{1,29},{2,6},{3,31},{4,8},{5,1},{6,10},{7,3},{8,12},{9,5},{1... | collective-permute-start | bytes 1585160 | tf_op jit(solution)/shard_map/ppermute | solution.py:105
  67.2 15.7 %collective-permute-start.15 = (bf16[16,16512]{1,0:T(8,128)(2,1)S(1)}, bf16[16,16512]{1,0:T(8,128)(2,1)S(1)}, u32[]{:S(2)}, u32[]{:S(2)}) collective-permute-start(bf16[16,16512]{1,0:T(8,128)(2,1)S(1)} %collective-permute-done.11.refs_12_), channel_id=1, source_target_pairs={{0,2},{1,3},{2,0},{3,1},{4,6},{5,7},{6,4},{7,5},{8,10},{9,11},{10,... | collective-permute-start | bytes 1585160 | tf_op jit(solution)/shard_map/ppermute | solution.py:105
  67.2 15.7 %collective-permute-start.17 = (bf16[16,16512]{1,0:T(8,128)(2,1)S(1)}, bf16[16,16512]{1,0:T(8,128)(2,1)S(1)}, u32[]{:S(2)}, u32[]{:S(2)}) collective-permute-start(bf16[16,16512]{1,0:T(8,128)(2,1)S(1)} %collective-permute-done.13.refs_15_), channel_id=1, source_target_pairs={{0,28},{1,5},{2,30},{3,7},{4,0},{5,9},{6,2},{7,11},{8,4},{9,13},{1... | collective-permute-start | bytes 1585160 | tf_op jit(solution)/shard_map/ppermute | solution.py:105
  70.7 3.9 %copy-start.1 = (bf16[1,184,27648]{2,1,0:T(8,128)(2,1)}, bf16[1,184,27648]{2,1,0:T(8,128)(2,1)S(1)}, u32[]{:S(2)}) copy-start(bf16[1,184,27648]{2,1,0:T(8,128)(2,1)S(1)} %collective-permute-done.2.refs_3_) | copy-start | bytes 30523396
  74.6 1.5 %copy-start = (bf16[1,184,5120]{2,1,0:T(8,128)(2,1)S(1)}, bf16[1,184,5120]{2,1,0:T(8,128)(2,1)}, u32[]{:S(2)}) copy-start(bf16[1,184,5120]{2,1,0:T(8,128)(2,1)} %refs_2_.1) | copy-start | bytes 5652484
  82.8 5.7 %copy-start.2 = (s32[184]{0:T(256)S(1)}, s32[184]{0:T(256)}, u32[]{:S(2)}) copy-start(s32[184]{0:T(256)} %param.8) | copy-start | bytes 2212
  88.4 1.8 %collective-permute-start.18 = (f32[2,184,256]{2,1,0:T(8,128)S(1)}, f32[2,184,256]{2,1,0:T(8,128)S(1)}, u32[]{:S(2)}, u32[]{:S(2)}) collective-permute-start(f32[2,184,256]{2,1,0:T(8,128)S(1)} %get-tuple-element.33), channel_id=1, source_target_pairs={{0,1},{1,0},{2,3},{3,2},{4,5},{5,4},{6,7},{7,6},{8,9},{9,8},{10,11... | collective-permute-start | bytes 1130504 | tf_op jit(solution)/shard_map/ppermute | solution.py:105
where the time goes:
time: 105 us
  waiting for transfers between devices  48.7 us (46%)
  starting transfers between devices  22.9 us (22%)
  blocking collectives  13.5 us (13%)
  Pallas kernels  10.8 us (10%)
  local copies, waits for them, and re-layouts  7.43 us (7%)
  other arithmetic  1.43 us (1%)
    ppermute x19, waiting for transfers between devices, mover(): return lambda block: lax.ppermute(block, both, pairs)  48.7 us
    ppermute x19, starting transfers between devices, mover(): return lambda block: lax.ppermute(block, both, pairs)  22.9 us
    all_to_all x1, blocking collectives, on_device(): return jnp.sum(lax.all_to_all(parts, 'section', 0, 0, tiled=True), axis=0)  13.5 us
    pallas_call x3, Pallas kernels, call(): pl.pallas_call(kernel, in_specs=[pl.BlockSpec(memory_space=space) for spa...  10.8 us
    unnamed x6, local copies, waits for them, and re-layouts  5.4 us
  transfers between devices with their start and end apart: 19, of which 10 were waited for; matrix products, arithmetic and copies ran while one was open for 3% of the time, Pallas kernels for 4%

commit v1 on v0

--- a/solution.py
+++ b/solution.py
@@ -10,7 +10,7 @@
 SEQ_DEV = 8
 VAL_SEQS = 16
 LANES = 128
-ACT_TILES = 2
+ACT_TILES = 1
 FETCH_MIB = 22
 LATE_MIB = 8
 MIRROR = (0, 2, 1, 4, 3, 6, 5, 7, 8, 10, 9, 14, 15, 13, 11, 12)
@@ -115,7 +115,7 @@
             lax.dynamic_slice_in_dim(grads[0], which * grad_width, grad_width, 1),
         ]
 
-    numbers = jnp.broadcast_to(val_ids.astype(jnp.bfloat16)[:, None], (SEQ_DEV, LANES))
+    numbers = jnp.broadcast_to(val_ids[:, None], (SEQ_DEV, LANES)).astype(jnp.bfloat16)
     mine = jnp.concatenate([*columns(val_acts, val_grads, core), numbers], axis=1)
     theirs = jnp.concatenate([*columns(val_acts, val_grads, 1 - core), numbers], axis=1)
     own, other = {}, {}

time: 105 us -> 105 us (level)
  no operation moved by 1% of the time
where the time goes in v1:
time: 105 us
  waiting for transfers between devices  48.7 us (46%)
  starting transfers between devices  22.9 us (22%)
  blocking collectives  13.5 us (13%)
  Pallas kernels  10.9 us (10%)
  local copies, waits for them, and re-layouts  7.43 us (7%)
  other arithmetic  1.43 us (1%)
    ppermute x19, waiting for transfers between devices, mover(): return lambda block: lax.ppermute(block, both, pairs)  48.7 us
    ppermute x19, starting transfers between devices, mover(): return lambda block: lax.ppermute(block, both, pairs)  22.9 us
    all_to_all x1, blocking collectives, on_device(): return jnp.sum(lax.all_to_all(parts, 'section', 0, 0, tiled=True), axis=0)  13.5 us
    pallas_call x3, Pallas kernels, call(): pl.pallas_call(kernel, in_specs=[pl.BlockSpec(memory_space=space) for spa...  10.9 us
    unnamed x6, local copies, waits for them, and re-layouts  5.4 us
  transfers between devices with their start and end apart: 19, of which 10 were waited for; matrix products, arithmetic and copies ran while one was open for 3% of the time, Pallas kernels for 4%

profile of v1, /device:TPU:8, one launch (start us, length us, event | category | flops | bytes accessed | tf_op | source)
XLA Modules:
  0.0 105.0 jit_solution(17704682374156684121)
XLA Ops:
  0.0 0.7 convert_element_type.4
  0.7 1.1 %dynamic-slice_bitcast_fusion.1 = (bf16[8,13824]{1,0:T(8,128)(2,1)S(1)}, bf16[8,13824]{1,0:T(8,128)(2,1)S(1)}) fusion(bf16[1,8,27648]{2,1,0:T(8,128)(2,1)} %param.9, s32[]{:T(128)S(6)} %select_n.25, s32[]{:T(128)S(6)} %select_n.27), kind=kLoop, calls=%fused_computation.6 | loop fusion | bytes 884744 | tf_op jit(solution)/shard_map/dynamic_slice | solution.py:114
  1.7 0.8 dynamic-slice_bitcast_fusion.3
  2.6 1.4 %collective-permute-done.refs_4_ = bf16[1,184,5120]{2,1,0:T(8,128)(2,1)S(1)} collective-permute-done((bf16[1,184,5120]{2,1,0:T(8,128)(2,1)}, bf16[1,184,5120]{2,1,0:T(8,128)(2,1)S(1)}, u32[]{:S(2)}, u32[]{:S(2)}) %collective-permute-start) | collective-permute-done | bytes 1884192 | tf_op jit(solution)/shard_map/ppermute | solution.py:105
  4.2 1.4 %collective-permute-done.1 = bf16[8,16512]{1,0:T(8,128)(2,1)S(1)} collective-permute-done((bf16[8,16512]{1,0:T(8,128)(2,1)S(1)}, bf16[8,16512]{1,0:T(8,128)(2,1)S(1)}, u32[]{:S(2)}, u32[]{:S(2)}) %collective-permute-start.1) | collective-permute-done | bytes 264224 | tf_op jit(solution)/shard_map/ppermute | solution.py:105
  5.8 0.2 collective-permute-start.2
  6.0 1.9 %collective-permute-start.3 = (bf16[16,16512]{1,0:T(8,128)(2,1)S(1)}, bf16[16,16512]{1,0:T(8,128)(2,1)S(1)}, u32[]{:S(2)}, u32[]{:S(2)}) collective-permute-start(bf16[16,16512]{1,0:T(8,128)(2,1)S(1)} %pad_maximum_fusion.refs_5_), channel_id=1, source_target_pairs={{0,4},{1,29},{2,6},{3,31},{4,8},{5,1},{6,10},{7,3},{8,12},{9,5},{1... | collective-permute-start | bytes 1585160 | tf_op jit(solution)/shard_map/ppermute | solution.py:105
  7.9 0.4 collective-permute-start.5
  8.4 4.0 %collective-permute-start.4 = (bf16[16,16512]{1,0:T(8,128)(2,1)S(1)}, bf16[16,16512]{1,0:T(8,128)(2,1)S(1)}, u32[]{:S(2)}, u32[]{:S(2)}) collective-permute-start(bf16[16,16512]{1,0:T(8,128)(2,1)S(1)} %pad_maximum_fusion.refs_5_), channel_id=1, source_target_pairs={{0,28},{1,5},{2,30},{3,7},{4,0},{5,9},{6,2},{7,11},{8,4},{9,13},{1... | collective-permute-start | bytes 1585160 | tf_op jit(solution)/shard_map/ppermute | solution.py:105
  12.4 9.8 %collective-permute-done.3.refs_6_ = bf16[16,16512]{1,0:T(8,128)(2,1)S(1)} collective-permute-done((bf16[16,16512]{1,0:T(8,128)(2,1)S(1)}, bf16[16,16512]{1,0:T(8,128)(2,1)S(1)}, u32[]{:S(2)}, u32[]{:S(2)}) %collective-permute-start.3) | collective-permute-done | bytes 528416 | tf_op jit(solution)/shard_map/ppermute | solution.py:105
  22.1 0.4 collective-permute-start.6
  22.5 1.2 %collective-permute-done.4.refs_7_ = bf16[16,16512]{1,0:T(8,128)(2,1)S(1)} collective-permute-done((bf16[16,16512]{1,0:T(8,128)(2,1)S(1)}, bf16[16,16512]{1,0:T(8,128)(2,1)S(1)}, u32[]{:S(2)}, u32[]{:S(2)}) %collective-permute-start.4) | collective-permute-done | bytes 528416 | tf_op jit(solution)/shard_map/ppermute | solution.py:105
  23.7 3.7 %collective-permute-start.7 = (bf16[16,16512]{1,0:T(8,128)(2,1)S(1)}, bf16[16,16512]{1,0:T(8,128)(2,1)S(1)}, u32[]{:S(2)}, u32[]{:S(2)}) collective-permute-start(bf16[16,16512]{1,0:T(8,128)(2,1)S(1)} %collective-permute-done.4.refs_7_), channel_id=1, source_target_pairs={{0,28},{1,5},{2,30},{3,7},{4,0},{5,9},{6,2},{7,11},{8,4},{9,13},{1... | collective-permute-start | bytes 1585160 | tf_op jit(solution)/shard_map/ppermute | solution.py:105
  27.3 0.4 collective-permute-start.10
  27.8 9.5 %collective-permute-done.6.refs_8_ = bf16[16,16512]{1,0:T(8,128)(2,1)S(1)} collective-permute-done((bf16[16,16512]{1,0:T(8,128)(2,1)S(1)}, bf16[16,16512]{1,0:T(8,128)(2,1)S(1)}, u32[]{:S(2)}, u32[]{:S(2)}) %collective-permute-start.6) | collective-permute-done | bytes 528416 | tf_op jit(solution)/shard_map/ppermute | solution.py:105
  37.3 1.0 collective-permute-done.7.refs_9_
  38.3 3.7 %collective-permute-start.9 = (bf16[16,16512]{1,0:T(8,128)(2,1)S(1)}, bf16[16,16512]{1,0:T(8,128)(2,1)S(1)}, u32[]{:S(2)}, u32[]{:S(2)}) collective-permute-start(bf16[16,16512]{1,0:T(8,128)(2,1)S(1)} %collective-permute-done.7.refs_9_), channel_id=1, source_target_pairs={{0,28},{1,5},{2,30},{3,7},{4,0},{5,9},{6,2},{7,11},{8,4},{9,13},{1... | collective-permute-start | bytes 1585160 | tf_op jit(solution)/shard_map/ppermute | solution.py:105
  42.0 0.4 collective-permute-start.12
  42.5 9.3 %collective-permute-done.8.refs_10_ = bf16[16,16512]{1,0:T(8,128)(2,1)S(1)} collective-permute-done((bf16[16,16512]{1,0:T(8,128)(2,1)S(1)}, bf16[16,16512]{1,0:T(8,128)(2,1)S(1)}, u32[]{:S(2)}, u32[]{:S(2)}) %collective-permute-start.8) | collective-permute-done | bytes 528416 | tf_op jit(solution)/shard_map/ppermute | solution.py:105
  51.8 0.5 collective-permute-start.14
  52.2 3.6 %collective-permute-start.13 = (bf16[16,16512]{1,0:T(8,128)(2,1)S(1)}, bf16[16,16512]{1,0:T(8,128)(2,1)S(1)}, u32[]{:S(2)}, u32[]{:S(2)}) collective-permute-start(bf16[16,16512]{1,0:T(8,128)(2,1)S(1)} %collective-permute-done.10.refs_16_), channel_id=1, source_target_pairs={{0,28},{1,5},{2,30},{3,7},{4,0},{5,9},{6,2},{7,11},{8,4},{9,13},{1... | collective-permute-start | bytes 1585160 | tf_op jit(solution)/shard_map/ppermute | solution.py:105
  55.8 11.4 %collective-permute-done.11.refs_12_ = bf16[16,16512]{1,0:T(8,128)(2,1)S(1)} collective-permute-done((bf16[16,16512]{1,0:T(8,128)(2,1)S(1)}, bf16[16,16512]{1,0:T(8,128)(2,1)S(1)}, u32[]{:S(2)}, u32[]{:S(2)}) %collective-permute-start.11) | collective-permute-done | bytes 528416 | tf_op jit(solution)/shard_map/ppermute | solution.py:105
  67.2 3.5 %collective-permute-start.17 = (bf16[16,16512]{1,0:T(8,128)(2,1)S(1)}, bf16[16,16512]{1,0:T(8,128)(2,1)S(1)}, u32[]{:S(2)}, u32[]{:S(2)}) collective-permute-start(bf16[16,16512]{1,0:T(8,128)(2,1)S(1)} %collective-permute-done.13.refs_15_), channel_id=1, source_target_pairs={{0,28},{1,5},{2,30},{3,7},{4,0},{5,9},{6,2},{7,11},{8,4},{9,13},{1... | collective-permute-start | bytes 1585160 | tf_op jit(solution)/shard_map/ppermute | solution.py:105
  70.7 3.9 %copy-done.1 = bf16[1,184,27648]{2,1,0:T(8,128)(2,1)} copy-done((bf16[1,184,27648]{2,1,0:T(8,128)(2,1)}, bf16[1,184,27648]{2,1,0:T(8,128)(2,1)S(1)}, u32[]{:S(2)}) %copy-start.1) | copy-done | bytes 10174488
  74.6 1.5 %copy-done = bf16[1,184,5120]{2,1,0:T(8,128)(2,1)S(1)} copy-done((bf16[1,184,5120]{2,1,0:T(8,128)(2,1)S(1)}, bf16[1,184,5120]{2,1,0:T(8,128)(2,1)}, u32[]{:S(2)}) %copy-start) | copy-done | bytes 1884184
  76.1 4.7 %shard_map.64 = (bf16[184,16384]{1,0:T(8,128)(2,1)S(1)}, bf16[184,16384]{1,0:T(8,128)(2,1)S(1)}, bf16[13,16,16512]{2,1,0:T(8,128)(2,1)S(1)}) custom-call(s32[1]{0:T(128)} %bitcast.1.refs_0_, bf16[1,184,27648]{2,1,0:T(8,128)(2,1)} %refs_1_.1, bf16[1,184,5120]{2,1,0:T(8,128)(2,1)S(1)} %copy-done, bf16[1,184,27648]{2,1,0:T(8,128)(2,1)} %copy-done.1, ...), custom_call_target="tpu_custom_call" | custom-call | tf_op jit(solution)/shard_map/pallas_call | solution.py:80
  80.8 2.1 %collective-permute-done.16.refs_1_ = bf16[16,16512]{1,0:T(8,128)(2,1)S(1)} collective-permute-done((bf16[16,16512]{1,0:T(8,128)(2,1)S(1)}, bf16[16,16512]{1,0:T(8,128)(2,1)S(1)}, u32[]{:S(2)}, u32[]{:S(2)}) %collective-permute-start.16) | collective-permute-done | bytes 528416 | tf_op jit(solution)/shard_map/ppermute | solution.py:105
  82.8 5.6 %shard_map.65 = (f32[2,184,256]{2,1,0:T(8,128)S(1)}, f32[2,184,256]{2,1,0:T(8,128)S(1)}, f32[256,16]{1,0:T(8,128)S(1)}) custom-call(bf16[184,16384]{1,0:T(8,128)(2,1)S(1)} %get-tuple-element.26.rows, bf16[184,16384]{1,0:T(8,128)(2,1)S(1)} %get-tuple-element.27.partner, bf16[13,16,16512]{2,1,0:T(8,128)(2,1)S(1)} %get-tuple-element.28.stack, ...), custom_call_target="tpu_custom_call" | custom-call | flops 3087007744 | tf_op jit(solution)/shard_map/pallas_call | solution.py:80
  88.6 1.7 %collective-permute-done.18.came = f32[2,184,256]{2,1,0:T(8,128)S(1)} collective-permute-done((f32[2,184,256]{2,1,0:T(8,128)S(1)}, f32[2,184,256]{2,1,0:T(8,128)S(1)}, u32[]{:S(2)}, u32[]{:S(2)}) %collective-permute-start.18) | collective-permute-done | bytes 376864 | tf_op jit(solution)/shard_map/ppermute | solution.py:105
  90.2 0.6 shard_map.66
  90.9 13.5 %all_to_all.5 = f32[8,8,2]{1,2,0:T(2,128)S(1)} all-to-all(f32[8,8,2]{1,2,0:T(2,128)S(1)} %bitcast.14), channel_id=1, replica_groups=mesh['section'=8,'zy'=16,'core'=2] {'section'}, dimensions={0} | all-to-all | bytes 1024 | tf_op jit(solution)/shard_map/all_to_all | solution.py:181
  104.4 0.6 reduce_sum.9
  (26 shorter events, 0.6 us)
Async XLA Ops:
  0.0 4.1 %collective-permute-start = (bf16[1,184,5120]{2,1,0:T(8,128)(2,1)}, bf16[1,184,5120]{2,1,0:T(8,128)(2,1)S(1)}, u32[]{:S(2)}, u32[]{:S(2)}) collective-permute-start(bf16[1,184,5120]{2,1,0:T(8,128)(2,1)} %refs_2_.1), channel_id=1, source_target_pairs={{0,1},{1,0},{2,3},{3,2},{4,5},{5,4},{6,7},{7,6},{8,9},{9,8},{10,11... | collective-permute-start | bytes 5652488 | tf_op jit(solution)/shard_map/ppermute | solution.py:105
  4.1 1.5 %collective-permute-start.1 = (bf16[8,16512]{1,0:T(8,128)(2,1)S(1)}, bf16[8,16512]{1,0:T(8,128)(2,1)S(1)}, u32[]{:S(2)}, u32[]{:S(2)}) collective-permute-start(bf16[8,16512]{1,0:T(8,128)(2,1)S(1)} %pad_maximum_fusion.1), channel_id=1, source_target_pairs={{0,1},{1,0},{2,3},{3,2},{4,5},{5,4},{6,7},{7,6},{8,9},{9,8},{10,11... | collective-permute-start | bytes 792584 | tf_op jit(solution)/shard_map/ppermute | solution.py:105
  5.8 64.9 %collective-permute-start.2 = (bf16[1,184,27648]{2,1,0:T(8,128)(2,1)}, bf16[1,184,27648]{2,1,0:T(8,128)(2,1)S(1)}, u32[]{:S(2)}, u32[]{:S(2)}) collective-permute-start(bf16[1,184,27648]{2,1,0:T(8,128)(2,1)} %refs_1_.1), channel_id=1, source_target_pairs={{0,1},{1,0},{2,3},{3,2},{4,5},{5,4},{6,7},{7,6},{8,9},{9,8},{10,11... | collective-permute-start | bytes 30523400 | tf_op jit(solution)/shard_map/ppermute | solution.py:105
  6.0 16.1 %collective-permute-start.3 = (bf16[16,16512]{1,0:T(8,128)(2,1)S(1)}, bf16[16,16512]{1,0:T(8,128)(2,1)S(1)}, u32[]{:S(2)}, u32[]{:S(2)}) collective-permute-start(bf16[16,16512]{1,0:T(8,128)(2,1)S(1)} %pad_maximum_fusion.refs_5_), channel_id=1, source_target_pairs={{0,4},{1,29},{2,6},{3,31},{4,8},{5,1},{6,10},{7,3},{8,12},{9,5},{1... | collective-permute-start | bytes 1585160 | tf_op jit(solution)/shard_map/ppermute | solution.py:105
  7.9 14.2 %collective-permute-start.5 = (bf16[16,16512]{1,0:T(8,128)(2,1)S(1)}, bf16[16,16512]{1,0:T(8,128)(2,1)S(1)}, u32[]{:S(2)}, u32[]{:S(2)}) collective-permute-start(bf16[16,16512]{1,0:T(8,128)(2,1)S(1)} %pad_maximum_fusion.refs_5_), channel_id=1, source_target_pairs={{0,2},{1,3},{2,0},{3,1},{4,6},{5,7},{6,4},{7,5},{8,10},{9,11},{10,... | collective-permute-start | bytes 1585160 | tf_op jit(solution)/shard_map/ppermute | solution.py:105
  8.4 15.3 %collective-permute-start.4 = (bf16[16,16512]{1,0:T(8,128)(2,1)S(1)}, bf16[16,16512]{1,0:T(8,128)(2,1)S(1)}, u32[]{:S(2)}, u32[]{:S(2)}) collective-permute-start(bf16[16,16512]{1,0:T(8,128)(2,1)S(1)} %pad_maximum_fusion.refs_5_), channel_id=1, source_target_pairs={{0,28},{1,5},{2,30},{3,7},{4,0},{5,9},{6,2},{7,11},{8,4},{9,13},{1... | collective-permute-start | bytes 1585160 | tf_op jit(solution)/shard_map/ppermute | solution.py:105
  22.1 15.2 %collective-permute-start.6 = (bf16[16,16512]{1,0:T(8,128)(2,1)S(1)}, bf16[16,16512]{1,0:T(8,128)(2,1)S(1)}, u32[]{:S(2)}, u32[]{:S(2)}) collective-permute-start(bf16[16,16512]{1,0:T(8,128)(2,1)S(1)} %collective-permute-done.3.refs_6_), channel_id=1, source_target_pairs={{0,4},{1,29},{2,6},{3,31},{4,8},{5,1},{6,10},{7,3},{8,12},{9,5},{1... | collective-permute-start | bytes 1585160 | tf_op jit(solution)/shard_map/ppermute | solution.py:105
  23.7 14.7 %collective-permute-start.7 = (bf16[16,16512]{1,0:T(8,128)(2,1)S(1)}, bf16[16,16512]{1,0:T(8,128)(2,1)S(1)}, u32[]{:S(2)}, u32[]{:S(2)}) collective-permute-start(bf16[16,16512]{1,0:T(8,128)(2,1)S(1)} %collective-permute-done.4.refs_7_), channel_id=1, source_target_pairs={{0,28},{1,5},{2,30},{3,7},{4,0},{5,9},{6,2},{7,11},{8,4},{9,13},{1... | collective-permute-start | bytes 1585160 | tf_op jit(solution)/shard_map/ppermute | solution.py:105
  27.3 15.1 %collective-permute-start.10 = (bf16[16,16512]{1,0:T(8,128)(2,1)S(1)}, bf16[16,16512]{1,0:T(8,128)(2,1)S(1)}, u32[]{:S(2)}, u32[]{:S(2)}) collective-permute-start(bf16[16,16512]{1,0:T(8,128)(2,1)S(1)} %collective-permute-done.4.refs_7_), channel_id=1, source_target_pairs={{0,2},{1,3},{2,0},{3,1},{4,6},{5,7},{6,4},{7,5},{8,10},{9,11},{10,... | collective-permute-start | bytes 1585160 | tf_op jit(solution)/shard_map/ppermute | solution.py:105
  37.3 14.5 %collective-permute-start.8 = (bf16[16,16512]{1,0:T(8,128)(2,1)S(1)}, bf16[16,16512]{1,0:T(8,128)(2,1)S(1)}, u32[]{:S(2)}, u32[]{:S(2)}) collective-permute-start(bf16[16,16512]{1,0:T(8,128)(2,1)S(1)} %collective-permute-done.6.refs_8_), channel_id=1, source_target_pairs={{0,4},{1,29},{2,6},{3,31},{4,8},{5,1},{6,10},{7,3},{8,12},{9,5},{1... | collective-permute-start | bytes 1585160 | tf_op jit(solution)/shard_map/ppermute | solution.py:105
  38.3 13.9 %collective-permute-start.9 = (bf16[16,16512]{1,0:T(8,128)(2,1)S(1)}, bf16[16,16512]{1,0:T(8,128)(2,1)S(1)}, u32[]{:S(2)}, u32[]{:S(2)}) collective-permute-start(bf16[16,16512]{1,0:T(8,128)(2,1)S(1)} %collective-permute-done.7.refs_9_), channel_id=1, source_target_pairs={{0,28},{1,5},{2,30},{3,7},{4,0},{5,9},{6,2},{7,11},{8,4},{9,13},{1... | collective-permute-start | bytes 1585160 | tf_op jit(solution)/shard_map/ppermute | solution.py:105
  42.0 13.8 %collective-permute-start.12 = (bf16[16,16512]{1,0:T(8,128)(2,1)S(1)}, bf16[16,16512]{1,0:T(8,128)(2,1)S(1)}, u32[]{:S(2)}, u32[]{:S(2)}) collective-permute-start(bf16[16,16512]{1,0:T(8,128)(2,1)S(1)} %collective-permute-done.6.refs_8_), channel_id=1, source_target_pairs={{0,2},{1,3},{2,0},{3,1},{4,6},{5,7},{6,4},{7,5},{8,10},{9,11},{10,... | collective-permute-start | bytes 1585160 | tf_op jit(solution)/shard_map/ppermute | solution.py:105
  51.8 15.4 %collective-permute-start.11 = (bf16[16,16512]{1,0:T(8,128)(2,1)S(1)}, bf16[16,16512]{1,0:T(8,128)(2,1)S(1)}, u32[]{:S(2)}, u32[]{:S(2)}) collective-permute-start(bf16[16,16512]{1,0:T(8,128)(2,1)S(1)} %collective-permute-done.8.refs_10_), channel_id=1, source_target_pairs={{0,4},{1,29},{2,6},{3,31},{4,8},{5,1},{6,10},{7,3},{8,12},{9,5},{1... | collective-permute-start | bytes 1585160 | tf_op jit(solution)/shard_map/ppermute | solution.py:105
  51.8 15.4 %collective-permute-start.14 = (bf16[16,16512]{1,0:T(8,128)(2,1)S(1)}, bf16[16,16512]{1,0:T(8,128)(2,1)S(1)}, u32[]{:S(2)}, u32[]{:S(2)}) collective-permute-start(bf16[16,16512]{1,0:T(8,128)(2,1)S(1)} %collective-permute-done.8.refs_10_), channel_id=1, source_target_pairs={{0,2},{1,3},{2,0},{3,1},{4,6},{5,7},{6,4},{7,5},{8,10},{9,11},{10,... | collective-permute-start | bytes 1585160 | tf_op jit(solution)/shard_map/ppermute | solution.py:105
  52.2 14.9 %collective-permute-start.13 = (bf16[16,16512]{1,0:T(8,128)(2,1)S(1)}, bf16[16,16512]{1,0:T(8,128)(2,1)S(1)}, u32[]{:S(2)}, u32[]{:S(2)}) collective-permute-start(bf16[16,16512]{1,0:T(8,128)(2,1)S(1)} %collective-permute-done.10.refs_16_), channel_id=1, source_target_pairs={{0,28},{1,5},{2,30},{3,7},{4,0},{5,9},{6,2},{7,11},{8,4},{9,13},{1... | collective-permute-start | bytes 1585160 | tf_op jit(solution)/shard_map/ppermute | solution.py:105
  67.2 15.7 %collective-permute-start.16 = (bf16[16,16512]{1,0:T(8,128)(2,1)S(1)}, bf16[16,16512]{1,0:T(8,128)(2,1)S(1)}, u32[]{:S(2)}, u32[]{:S(2)}) collective-permute-start(bf16[16,16512]{1,0:T(8,128)(2,1)S(1)} %collective-permute-done.5.refs_13_), channel_id=1, source_target_pairs={{0,4},{1,29},{2,6},{3,31},{4,8},{5,1},{6,10},{7,3},{8,12},{9,5},{1... | collective-permute-start | bytes 1585160 | tf_op jit(solution)/shard_map/ppermute | solution.py:105
  67.2 15.7 %collective-permute-start.15 = (bf16[16,16512]{1,0:T(8,128)(2,1)S(1)}, bf16[16,16512]{1,0:T(8,128)(2,1)S(1)}, u32[]{:S(2)}, u32[]{:S(2)}) collective-permute-start(bf16[16,16512]{1,0:T(8,128)(2,1)S(1)} %collective-permute-done.11.refs_12_), channel_id=1, source_target_pairs={{0,2},{1,3},{2,0},{3,1},{4,6},{5,7},{6,4},{7,5},{8,10},{9,11},{10,... | collective-permute-start | bytes 1585160 | tf_op jit(solution)/shard_map/ppermute | solution.py:105
  67.2 15.7 %collective-permute-start.17 = (bf16[16,16512]{1,0:T(8,128)(2,1)S(1)}, bf16[16,16512]{1,0:T(8,128)(2,1)S(1)}, u32[]{:S(2)}, u32[]{:S(2)}) collective-permute-start(bf16[16,16512]{1,0:T(8,128)(2,1)S(1)} %collective-permute-done.13.refs_15_), channel_id=1, source_target_pairs={{0,28},{1,5},{2,30},{3,7},{4,0},{5,9},{6,2},{7,11},{8,4},{9,13},{1... | collective-permute-start | bytes 1585160 | tf_op jit(solution)/shard_map/ppermute | solution.py:105
  70.7 3.9 %copy-start.1 = (bf16[1,184,27648]{2,1,0:T(8,128)(2,1)}, bf16[1,184,27648]{2,1,0:T(8,128)(2,1)S(1)}, u32[]{:S(2)}) copy-start(bf16[1,184,27648]{2,1,0:T(8,128)(2,1)S(1)} %collective-permute-done.2.refs_3_) | copy-start | bytes 30523396
  74.6 1.5 %copy-start = (bf16[1,184,5120]{2,1,0:T(8,128)(2,1)S(1)}, bf16[1,184,5120]{2,1,0:T(8,128)(2,1)}, u32[]{:S(2)}) copy-start(bf16[1,184,5120]{2,1,0:T(8,128)(2,1)} %refs_2_.1) | copy-start | bytes 5652484
  82.8 5.7 %copy-start.2 = (s32[184]{0:T(256)S(1)}, s32[184]{0:T(256)}, u32[]{:S(2)}) copy-start(s32[184]{0:T(256)} %param.8) | copy-start | bytes 2212
  88.4 1.8 %collective-permute-start.18 = (f32[2,184,256]{2,1,0:T(8,128)S(1)}, f32[2,184,256]{2,1,0:T(8,128)S(1)}, u32[]{:S(2)}, u32[]{:S(2)}) collective-permute-start(f32[2,184,256]{2,1,0:T(8,128)S(1)} %get-tuple-element.33), channel_id=1, source_target_pairs={{0,1},{1,0},{2,3},{3,2},{4,5},{5,4},{6,7},{7,6},{8,9},{9,8},{10,11... | collective-permute-start | bytes 1130504 | tf_op jit(solution)/shard_map/ppermute | solution.py:105

commit v2 on v1

--- a/solution.py
+++ b/solution.py
@@ -130,10 +130,10 @@
     own[-1] = ahead(own[0])
     other[0] = beside(own[0])
     own[1] = back(own[0])
-    own[-2] = ahead(after(own[-1], other[0]))
+    own[-2] = ahead(own[-1])
     other[1] = beside(own[1])
     own[2] = back(own[1])
-    own[-3] = ahead(own[-2])
+    own[-3] = ahead(after(own[-2], other[0]))
     other[-2] = beside(after(own[-2], other[0]))
     own[3] = back(own[2])
     own[4] = ahead(after(own[-3], other[1]))

time: 105 us -> 105 us (level)
  no operation moved by 1% of the time
where the time goes in v2:
time: 105 us
  waiting for transfers between devices  49.4 us (47%)
  starting transfers between devices  22.3 us (21%)
  blocking collectives  13.5 us (13%)
  Pallas kernels  10.9 us (10%)
  local copies, waits for them, and re-layouts  7.43 us (7%)
  other arithmetic  1.43 us (1%)
    ppermute x19, waiting for transfers between devices, mover(): return lambda block: lax.ppermute(block, both, pairs)  49.4 us
    ppermute x19, starting transfers between devices, mover(): return lambda block: lax.ppermute(block, both, pairs)  22.3 us
    all_to_all x1, blocking collectives, on_device(): return jnp.sum(lax.all_to_all(parts, 'section', 0, 0, tiled=True), axis=0)  13.5 us
    pallas_call x3, Pallas kernels, call(): pl.pallas_call(kernel, in_specs=[pl.BlockSpec(memory_space=space) for spa...  10.9 us
    unnamed x6, local copies, waits for them, and re-layouts  5.4 us
  transfers between devices with their start and end apart: 19, of which 10 were waited for; matrix products, arithmetic and copies ran while one was open for 3% of the time, Pallas kernels for 4%

profile of v2, /device:TPU:8, one launch (start us, length us, event | category | flops | bytes accessed | tf_op | source)
XLA Modules:
  0.0 105.0 jit_solution(14747276380296844753)
XLA Ops:
  0.0 0.7 convert_element_type.4
  0.7 1.1 %dynamic-slice_bitcast_fusion.1 = (bf16[8,13824]{1,0:T(8,128)(2,1)S(1)}, bf16[8,13824]{1,0:T(8,128)(2,1)S(1)}) fusion(bf16[1,8,27648]{2,1,0:T(8,128)(2,1)} %param.9, s32[]{:T(128)S(6)} %select_n.25, s32[]{:T(128)S(6)} %select_n.27), kind=kLoop, calls=%fused_computation.6 | loop fusion | bytes 884744 | tf_op jit(solution)/shard_map/dynamic_slice | solution.py:114
  1.7 0.8 dynamic-slice_bitcast_fusion.3
  2.6 1.4 %collective-permute-done.refs_4_ = bf16[1,184,5120]{2,1,0:T(8,128)(2,1)S(1)} collective-permute-done((bf16[1,184,5120]{2,1,0:T(8,128)(2,1)}, bf16[1,184,5120]{2,1,0:T(8,128)(2,1)S(1)}, u32[]{:S(2)}, u32[]{:S(2)}) %collective-permute-start) | collective-permute-done | bytes 1884192 | tf_op jit(solution)/shard_map/ppermute | solution.py:105
  4.1 0.1 collective-permute-start.1
  4.2 1.4 %collective-permute-done.1 = bf16[8,16512]{1,0:T(8,128)(2,1)S(1)} collective-permute-done((bf16[8,16512]{1,0:T(8,128)(2,1)S(1)}, bf16[8,16512]{1,0:T(8,128)(2,1)S(1)}, u32[]{:S(2)}, u32[]{:S(2)}) %collective-permute-start.1) | collective-permute-done | bytes 264224 | tf_op jit(solution)/shard_map/ppermute | solution.py:105
  5.8 0.2 collective-permute-start.2
  6.0 1.9 %collective-permute-start.3 = (bf16[16,16512]{1,0:T(8,128)(2,1)S(1)}, bf16[16,16512]{1,0:T(8,128)(2,1)S(1)}, u32[]{:S(2)}, u32[]{:S(2)}) collective-permute-start(bf16[16,16512]{1,0:T(8,128)(2,1)S(1)} %pad_maximum_fusion.refs_5_), channel_id=1, source_target_pairs={{0,4},{1,29},{2,6},{3,31},{4,8},{5,1},{6,10},{7,3},{8,12},{9,5},{1... | collective-permute-start | bytes 1585160 | tf_op jit(solution)/shard_map/ppermute | solution.py:105
  7.9 4.0 %collective-permute-start.4 = (bf16[16,16512]{1,0:T(8,128)(2,1)S(1)}, bf16[16,16512]{1,0:T(8,128)(2,1)S(1)}, u32[]{:S(2)}, u32[]{:S(2)}) collective-permute-start(bf16[16,16512]{1,0:T(8,128)(2,1)S(1)} %pad_maximum_fusion.refs_5_), channel_id=1, source_target_pairs={{0,28},{1,5},{2,30},{3,7},{4,0},{5,9},{6,2},{7,11},{8,4},{9,13},{1... | collective-permute-start | bytes 1585160 | tf_op jit(solution)/shard_map/ppermute | solution.py:105
  11.9 0.4 collective-permute-start.7
  12.3 9.9 %collective-permute-done.3.refs_6_ = bf16[16,16512]{1,0:T(8,128)(2,1)S(1)} collective-permute-done((bf16[16,16512]{1,0:T(8,128)(2,1)S(1)}, bf16[16,16512]{1,0:T(8,128)(2,1)S(1)}, u32[]{:S(2)}, u32[]{:S(2)}) %collective-permute-start.3) | collective-permute-done | bytes 528416 | tf_op jit(solution)/shard_map/ppermute | solution.py:105
  22.3 1.4 %collective-permute-done.4.refs_7_ = bf16[16,16512]{1,0:T(8,128)(2,1)S(1)} collective-permute-done((bf16[16,16512]{1,0:T(8,128)(2,1)S(1)}, bf16[16,16512]{1,0:T(8,128)(2,1)S(1)}, u32[]{:S(2)}, u32[]{:S(2)}) %collective-permute-start.4) | collective-permute-done | bytes 528416 | tf_op jit(solution)/shard_map/ppermute | solution.py:105
  23.7 3.7 %collective-permute-start.6 = (bf16[16,16512]{1,0:T(8,128)(2,1)S(1)}, bf16[16,16512]{1,0:T(8,128)(2,1)S(1)}, u32[]{:S(2)}, u32[]{:S(2)}) collective-permute-start(bf16[16,16512]{1,0:T(8,128)(2,1)S(1)} %collective-permute-done.4.refs_7_), channel_id=1, source_target_pairs={{0,28},{1,5},{2,30},{3,7},{4,0},{5,9},{6,2},{7,11},{8,4},{9,13},{1... | collective-permute-start | bytes 1585160 | tf_op jit(solution)/shard_map/ppermute | solution.py:105
  27.3 0.4 collective-permute-start.10
  27.8 9.3 %collective-permute-done.5.refs_8_ = bf16[16,16512]{1,0:T(8,128)(2,1)S(1)} collective-permute-done((bf16[16,16512]{1,0:T(8,128)(2,1)S(1)}, bf16[16,16512]{1,0:T(8,128)(2,1)S(1)}, u32[]{:S(2)}, u32[]{:S(2)}) %collective-permute-start.5) | collective-permute-done | bytes 528416 | tf_op jit(solution)/shard_map/ppermute | solution.py:105
  37.1 1.2 %collective-permute-done.6.refs_9_ = bf16[16,16512]{1,0:T(8,128)(2,1)S(1)} collective-permute-done((bf16[16,16512]{1,0:T(8,128)(2,1)S(1)}, bf16[16,16512]{1,0:T(8,128)(2,1)S(1)}, u32[]{:S(2)}, u32[]{:S(2)}) %collective-permute-start.6) | collective-permute-done | bytes 528416 | tf_op jit(solution)/shard_map/ppermute | solution.py:105
  38.3 3.7 %collective-permute-start.9 = (bf16[16,16512]{1,0:T(8,128)(2,1)S(1)}, bf16[16,16512]{1,0:T(8,128)(2,1)S(1)}, u32[]{:S(2)}, u32[]{:S(2)}) collective-permute-start(bf16[16,16512]{1,0:T(8,128)(2,1)S(1)} %collective-permute-done.6.refs_9_), channel_id=1, source_target_pairs={{0,28},{1,5},{2,30},{3,7},{4,0},{5,9},{6,2},{7,11},{8,4},{9,13},{1... | collective-permute-start | bytes 1585160 | tf_op jit(solution)/shard_map/ppermute | solution.py:105
  42.0 0.4 collective-permute-start.12
  42.5 9.3 %collective-permute-done.8.refs_10_ = bf16[16,16512]{1,0:T(8,128)(2,1)S(1)} collective-permute-done((bf16[16,16512]{1,0:T(8,128)(2,1)S(1)}, bf16[16,16512]{1,0:T(8,128)(2,1)S(1)}, u32[]{:S(2)}, u32[]{:S(2)}) %collective-permute-start.8) | collective-permute-done | bytes 528416 | tf_op jit(solution)/shard_map/ppermute | solution.py:105
  51.8 0.5 collective-permute-start.14
  52.3 3.5 %collective-permute-start.13 = (bf16[16,16512]{1,0:T(8,128)(2,1)S(1)}, bf16[16,16512]{1,0:T(8,128)(2,1)S(1)}, u32[]{:S(2)}, u32[]{:S(2)}) collective-permute-start(bf16[16,16512]{1,0:T(8,128)(2,1)S(1)} %collective-permute-done.10.refs_16_), channel_id=1, source_target_pairs={{0,28},{1,5},{2,30},{3,7},{4,0},{5,9},{6,2},{7,11},{8,4},{9,13},{1... | collective-permute-start | bytes 1585160 | tf_op jit(solution)/shard_map/ppermute | solution.py:105
  55.7 11.5 %collective-permute-done.11.refs_12_ = bf16[16,16512]{1,0:T(8,128)(2,1)S(1)} collective-permute-done((bf16[16,16512]{1,0:T(8,128)(2,1)S(1)}, bf16[16,16512]{1,0:T(8,128)(2,1)S(1)}, u32[]{:S(2)}, u32[]{:S(2)}) %collective-permute-start.11) | collective-permute-done | bytes 528416 | tf_op jit(solution)/shard_map/ppermute | solution.py:105
  67.2 3.2 %collective-permute-start.17 = (bf16[16,16512]{1,0:T(8,128)(2,1)S(1)}, bf16[16,16512]{1,0:T(8,128)(2,1)S(1)}, u32[]{:S(2)}, u32[]{:S(2)}) collective-permute-start(bf16[16,16512]{1,0:T(8,128)(2,1)S(1)} %collective-permute-done.13.refs_15_), channel_id=1, source_target_pairs={{0,28},{1,5},{2,30},{3,7},{4,0},{5,9},{6,2},{7,11},{8,4},{9,13},{1... | collective-permute-start | bytes 1585160 | tf_op jit(solution)/shard_map/ppermute | solution.py:105
  70.5 3.9 %copy-done.1 = bf16[1,184,27648]{2,1,0:T(8,128)(2,1)} copy-done((bf16[1,184,27648]{2,1,0:T(8,128)(2,1)}, bf16[1,184,27648]{2,1,0:T(8,128)(2,1)S(1)}, u32[]{:S(2)}) %copy-start.1) | copy-done | bytes 10174488
  74.3 1.5 %copy-done = bf16[1,184,5120]{2,1,0:T(8,128)(2,1)S(1)} copy-done((bf16[1,184,5120]{2,1,0:T(8,128)(2,1)S(1)}, bf16[1,184,5120]{2,1,0:T(8,128)(2,1)}, u32[]{:S(2)}) %copy-start) | copy-done | bytes 1884184
  75.9 4.7 %shard_map.64 = (bf16[184,16384]{1,0:T(8,128)(2,1)S(1)}, bf16[184,16384]{1,0:T(8,128)(2,1)S(1)}, bf16[13,16,16512]{2,1,0:T(8,128)(2,1)S(1)}) custom-call(s32[1]{0:T(128)} %bitcast.1.refs_0_, bf16[1,184,27648]{2,1,0:T(8,128)(2,1)} %refs_1_.1, bf16[1,184,5120]{2,1,0:T(8,128)(2,1)S(1)} %copy-done, bf16[1,184,27648]{2,1,0:T(8,128)(2,1)} %copy-done.1, ...), custom_call_target="tpu_custom_call" | custom-call | tf_op jit(solution)/shard_map/pallas_call | solution.py:80
  80.6 2.3 %collective-permute-done.16.refs_1_ = bf16[16,16512]{1,0:T(8,128)(2,1)S(1)} collective-permute-done((bf16[16,16512]{1,0:T(8,128)(2,1)S(1)}, bf16[16,16512]{1,0:T(8,128)(2,1)S(1)}, u32[]{:S(2)}, u32[]{:S(2)}) %collective-permute-start.16) | collective-permute-done | bytes 528416 | tf_op jit(solution)/shard_map/ppermute | solution.py:105
  82.9 5.6 %shard_map.65 = (f32[2,184,256]{2,1,0:T(8,128)S(1)}, f32[2,184,256]{2,1,0:T(8,128)S(1)}, f32[256,16]{1,0:T(8,128)S(1)}) custom-call(bf16[184,16384]{1,0:T(8,128)(2,1)S(1)} %get-tuple-element.24.rows, bf16[184,16384]{1,0:T(8,128)(2,1)S(1)} %get-tuple-element.25.partner, bf16[13,16,16512]{2,1,0:T(8,128)(2,1)S(1)} %get-tuple-element.26.stack, ...), custom_call_target="tpu_custom_call" | custom-call | flops 3087007744 | tf_op jit(solution)/shard_map/pallas_call | solution.py:80
  88.5 1.7 %collective-permute-done.18.came = f32[2,184,256]{2,1,0:T(8,128)S(1)} collective-permute-done((f32[2,184,256]{2,1,0:T(8,128)S(1)}, f32[2,184,256]{2,1,0:T(8,128)S(1)}, u32[]{:S(2)}, u32[]{:S(2)}) %collective-permute-start.18) | collective-permute-done | bytes 376864 | tf_op jit(solution)/shard_map/ppermute | solution.py:105
  90.2 0.6 shard_map.66
  90.9 13.5 %all_to_all.5 = f32[8,8,2]{1,2,0:T(2,128)S(1)} all-to-all(f32[8,8,2]{1,2,0:T(2,128)S(1)} %bitcast.14), channel_id=1, replica_groups=mesh['section'=8,'zy'=16,'core'=2] {'section'}, dimensions={0} | all-to-all | bytes 1024 | tf_op jit(solution)/shard_map/all_to_all | solution.py:181
  104.4 0.6 reduce_sum.9
  (26 shorter events, 0.5 us)
Async XLA Ops:
  0.0 4.1 %collective-permute-start = (bf16[1,184,5120]{2,1,0:T(8,128)(2,1)}, bf16[1,184,5120]{2,1,0:T(8,128)(2,1)S(1)}, u32[]{:S(2)}, u32[]{:S(2)}) collective-permute-start(bf16[1,184,5120]{2,1,0:T(8,128)(2,1)} %refs_2_.1), channel_id=1, source_target_pairs={{0,1},{1,0},{2,3},{3,2},{4,5},{5,4},{6,7},{7,6},{8,9},{9,8},{10,11... | collective-permute-start | bytes 5652488 | tf_op jit(solution)/shard_map/ppermute | solution.py:105
  4.1 1.5 %collective-permute-start.1 = (bf16[8,16512]{1,0:T(8,128)(2,1)S(1)}, bf16[8,16512]{1,0:T(8,128)(2,1)S(1)}, u32[]{:S(2)}, u32[]{:S(2)}) collective-permute-start(bf16[8,16512]{1,0:T(8,128)(2,1)S(1)} %pad_maximum_fusion.1), channel_id=1, source_target_pairs={{0,1},{1,0},{2,3},{3,2},{4,5},{5,4},{6,7},{7,6},{8,9},{9,8},{10,11... | collective-permute-start | bytes 792584 | tf_op jit(solution)/shard_map/ppermute | solution.py:105
  5.8 64.7 %collective-permute-start.2 = (bf16[1,184,27648]{2,1,0:T(8,128)(2,1)}, bf16[1,184,27648]{2,1,0:T(8,128)(2,1)S(1)}, u32[]{:S(2)}, u32[]{:S(2)}) collective-permute-start(bf16[1,184,27648]{2,1,0:T(8,128)(2,1)} %refs_1_.1), channel_id=1, source_target_pairs={{0,1},{1,0},{2,3},{3,2},{4,5},{5,4},{6,7},{7,6},{8,9},{9,8},{10,11... | collective-permute-start | bytes 30523400 | tf_op jit(solution)/shard_map/ppermute | solution.py:105
  6.0 16.3 %collective-permute-start.3 = (bf16[16,16512]{1,0:T(8,128)(2,1)S(1)}, bf16[16,16512]{1,0:T(8,128)(2,1)S(1)}, u32[]{:S(2)}, u32[]{:S(2)}) collective-permute-start(bf16[16,16512]{1,0:T(8,128)(2,1)S(1)} %pad_maximum_fusion.refs_5_), channel_id=1, source_target_pairs={{0,4},{1,29},{2,6},{3,31},{4,8},{5,1},{6,10},{7,3},{8,12},{9,5},{1... | collective-permute-start | bytes 1585160 | tf_op jit(solution)/shard_map/ppermute | solution.py:105
  7.9 15.7 %collective-permute-start.4 = (bf16[16,16512]{1,0:T(8,128)(2,1)S(1)}, bf16[16,16512]{1,0:T(8,128)(2,1)S(1)}, u32[]{:S(2)}, u32[]{:S(2)}) collective-permute-start(bf16[16,16512]{1,0:T(8,128)(2,1)S(1)} %pad_maximum_fusion.refs_5_), channel_id=1, source_target_pairs={{0,28},{1,5},{2,30},{3,7},{4,0},{5,9},{6,2},{7,11},{8,4},{9,13},{1... | collective-permute-start | bytes 1585160 | tf_op jit(solution)/shard_map/ppermute | solution.py:105
  11.9 15.9 %collective-permute-start.7 = (bf16[16,16512]{1,0:T(8,128)(2,1)S(1)}, bf16[16,16512]{1,0:T(8,128)(2,1)S(1)}, u32[]{:S(2)}, u32[]{:S(2)}) collective-permute-start(bf16[16,16512]{1,0:T(8,128)(2,1)S(1)} %pad_maximum_fusion.refs_5_), channel_id=1, source_target_pairs={{0,2},{1,3},{2,0},{3,1},{4,6},{5,7},{6,4},{7,5},{8,10},{9,11},{10,... | collective-permute-start | bytes 1585160 | tf_op jit(solution)/shard_map/ppermute | solution.py:105
  22.3 14.8 %collective-permute-start.5 = (bf16[16,16512]{1,0:T(8,128)(2,1)S(1)}, bf16[16,16512]{1,0:T(8,128)(2,1)S(1)}, u32[]{:S(2)}, u32[]{:S(2)}) collective-permute-start(bf16[16,16512]{1,0:T(8,128)(2,1)S(1)} %collective-permute-done.3.refs_6_), channel_id=1, source_target_pairs={{0,4},{1,29},{2,6},{3,31},{4,8},{5,1},{6,10},{7,3},{8,12},{9,5},{1... | collective-permute-start | bytes 1585160 | tf_op jit(solution)/shard_map/ppermute | solution.py:105
  23.7 14.7 %collective-permute-start.6 = (bf16[16,16512]{1,0:T(8,128)(2,1)S(1)}, bf16[16,16512]{1,0:T(8,128)(2,1)S(1)}, u32[]{:S(2)}, u32[]{:S(2)}) collective-permute-start(bf16[16,16512]{1,0:T(8,128)(2,1)S(1)} %collective-permute-done.4.refs_7_), channel_id=1, source_target_pairs={{0,28},{1,5},{2,30},{3,7},{4,0},{5,9},{6,2},{7,11},{8,4},{9,13},{1... | collective-permute-start | bytes 1585160 | tf_op jit(solution)/shard_map/ppermute | solution.py:105
  27.3 15.1 %collective-permute-start.10 = (bf16[16,16512]{1,0:T(8,128)(2,1)S(1)}, bf16[16,16512]{1,0:T(8,128)(2,1)S(1)}, u32[]{:S(2)}, u32[]{:S(2)}) collective-permute-start(bf16[16,16512]{1,0:T(8,128)(2,1)S(1)} %collective-permute-done.4.refs_7_), channel_id=1, source_target_pairs={{0,2},{1,3},{2,0},{3,1},{4,6},{5,7},{6,4},{7,5},{8,10},{9,11},{10,... | collective-permute-start | bytes 1585160 | tf_op jit(solution)/shard_map/ppermute | solution.py:105
  37.1 14.7 %collective-permute-start.8 = (bf16[16,16512]{1,0:T(8,128)(2,1)S(1)}, bf16[16,16512]{1,0:T(8,128)(2,1)S(1)}, u32[]{:S(2)}, u32[]{:S(2)}) collective-permute-start(bf16[16,16512]{1,0:T(8,128)(2,1)S(1)} %collective-permute-done.5.refs_8_), channel_id=1, source_target_pairs={{0,4},{1,29},{2,6},{3,31},{4,8},{5,1},{6,10},{7,3},{8,12},{9,5},{1... | collective-permute-start | bytes 1585160 | tf_op jit(solution)/shard_map/ppermute | solution.py:105
  38.3 13.9 %collective-permute-start.9 = (bf16[16,16512]{1,0:T(8,128)(2,1)S(1)}, bf16[16,16512]{1,0:T(8,128)(2,1)S(1)}, u32[]{:S(2)}, u32[]{:S(2)}) collective-permute-start(bf16[16,16512]{1,0:T(8,128)(2,1)S(1)} %collective-permute-done.6.refs_9_), channel_id=1, source_target_pairs={{0,28},{1,5},{2,30},{3,7},{4,0},{5,9},{6,2},{7,11},{8,4},{9,13},{1... | collective-permute-start | bytes 1585160 | tf_op jit(solution)/shard_map/ppermute | solution.py:105
  42.0 13.7 %collective-permute-start.12 = (bf16[16,16512]{1,0:T(8,128)(2,1)S(1)}, bf16[16,16512]{1,0:T(8,128)(2,1)S(1)}, u32[]{:S(2)}, u32[]{:S(2)}) collective-permute-start(bf16[16,16512]{1,0:T(8,128)(2,1)S(1)} %collective-permute-done.5.refs_8_), channel_id=1, source_target_pairs={{0,2},{1,3},{2,0},{3,1},{4,6},{5,7},{6,4},{7,5},{8,10},{9,11},{10,... | collective-permute-start | bytes 1585160 | tf_op jit(solution)/shard_map/ppermute | solution.py:105
  51.8 15.4 %collective-permute-start.11 = (bf16[16,16512]{1,0:T(8,128)(2,1)S(1)}, bf16[16,16512]{1,0:T(8,128)(2,1)S(1)}, u32[]{:S(2)}, u32[]{:S(2)}) collective-permute-start(bf16[16,16512]{1,0:T(8,128)(2,1)S(1)} %collective-permute-done.8.refs_10_), channel_id=1, source_target_pairs={{0,4},{1,29},{2,6},{3,31},{4,8},{5,1},{6,10},{7,3},{8,12},{9,5},{1... | collective-permute-start | bytes 1585160 | tf_op jit(solution)/shard_map/ppermute | solution.py:105
  51.8 15.4 %collective-permute-start.14 = (bf16[16,16512]{1,0:T(8,128)(2,1)S(1)}, bf16[16,16512]{1,0:T(8,128)(2,1)S(1)}, u32[]{:S(2)}, u32[]{:S(2)}) collective-permute-start(bf16[16,16512]{1,0:T(8,128)(2,1)S(1)} %collective-permute-done.8.refs_10_), channel_id=1, source_target_pairs={{0,2},{1,3},{2,0},{3,1},{4,6},{5,7},{6,4},{7,5},{8,10},{9,11},{10,... | collective-permute-start | bytes 1585160 | tf_op jit(solution)/shard_map/ppermute | solution.py:105
  52.3 15.0 %collective-permute-start.13 = (bf16[16,16512]{1,0:T(8,128)(2,1)S(1)}, bf16[16,16512]{1,0:T(8,128)(2,1)S(1)}, u32[]{:S(2)}, u32[]{:S(2)}) collective-permute-start(bf16[16,16512]{1,0:T(8,128)(2,1)S(1)} %collective-permute-done.10.refs_16_), channel_id=1, source_target_pairs={{0,28},{1,5},{2,30},{3,7},{4,0},{5,9},{6,2},{7,11},{8,4},{9,13},{1... | collective-permute-start | bytes 1585160 | tf_op jit(solution)/shard_map/ppermute | solution.py:105
  67.2 15.6 %collective-permute-start.16 = (bf16[16,16512]{1,0:T(8,128)(2,1)S(1)}, bf16[16,16512]{1,0:T(8,128)(2,1)S(1)}, u32[]{:S(2)}, u32[]{:S(2)}) collective-permute-start(bf16[16,16512]{1,0:T(8,128)(2,1)S(1)} %collective-permute-done.7.refs_13_), channel_id=1, source_target_pairs={{0,4},{1,29},{2,6},{3,31},{4,8},{5,1},{6,10},{7,3},{8,12},{9,5},{1... | collective-permute-start | bytes 1585160 | tf_op jit(solution)/shard_map/ppermute | solution.py:105
  67.2 15.6 %collective-permute-start.17 = (bf16[16,16512]{1,0:T(8,128)(2,1)S(1)}, bf16[16,16512]{1,0:T(8,128)(2,1)S(1)}, u32[]{:S(2)}, u32[]{:S(2)}) collective-permute-start(bf16[16,16512]{1,0:T(8,128)(2,1)S(1)} %collective-permute-done.13.refs_15_), channel_id=1, source_target_pairs={{0,28},{1,5},{2,30},{3,7},{4,0},{5,9},{6,2},{7,11},{8,4},{9,13},{1... | collective-permute-start | bytes 1585160 | tf_op jit(solution)/shard_map/ppermute | solution.py:105
  70.5 12.4 %collective-permute-start.15 = (bf16[16,16512]{1,0:T(8,128)(2,1)S(1)}, bf16[16,16512]{1,0:T(8,128)(2,1)S(1)}, u32[]{:S(2)}, u32[]{:S(2)}) collective-permute-start(bf16[16,16512]{1,0:T(8,128)(2,1)S(1)} %collective-permute-done.11.refs_12_), channel_id=1, source_target_pairs={{0,2},{1,3},{2,0},{3,1},{4,6},{5,7},{6,4},{7,5},{8,10},{9,11},{10,... | collective-permute-start | bytes 1585160 | tf_op jit(solution)/shard_map/ppermute | solution.py:105
  70.5 3.9 %copy-start.1 = (bf16[1,184,27648]{2,1,0:T(8,128)(2,1)}, bf16[1,184,27648]{2,1,0:T(8,128)(2,1)S(1)}, u32[]{:S(2)}) copy-start(bf16[1,184,27648]{2,1,0:T(8,128)(2,1)S(1)} %collective-permute-done.2.refs_3_) | copy-start | bytes 30523396
  74.3 1.5 %copy-start = (bf16[1,184,5120]{2,1,0:T(8,128)(2,1)S(1)}, bf16[1,184,5120]{2,1,0:T(8,128)(2,1)}, u32[]{:S(2)}) copy-start(bf16[1,184,5120]{2,1,0:T(8,128)(2,1)} %refs_2_.1) | copy-start | bytes 5652484
  82.8 5.7 %copy-start.2 = (s32[184]{0:T(256)S(1)}, s32[184]{0:T(256)}, u32[]{:S(2)}) copy-start(s32[184]{0:T(256)} %param.8) | copy-start | bytes 2212
  88.4 1.8 %collective-permute-start.18 = (f32[2,184,256]{2,1,0:T(8,128)S(1)}, f32[2,184,256]{2,1,0:T(8,128)S(1)}, u32[]{:S(2)}, u32[]{:S(2)}) collective-permute-start(f32[2,184,256]{2,1,0:T(8,128)S(1)} %get-tuple-element.31), channel_id=1, source_target_pairs={{0,1},{1,0},{2,3},{3,2},{4,5},{5,4},{6,7},{7,6},{8,9},{9,8},{10,11... | collective-permute-start | bytes 1130504 | tf_op jit(solution)/shard_map/ppermute | solution.py:105
